TPU v7x, 128 devices: a whole 4x4x4 slice. The times are simulated.
128 devices in a mesh: grp: 4 (over y_hi, core), pan: 32 (over x, y_lo, z).
Axes of the slice: x: 4, y: 4 (y_hi: 2, y_lo: 2; y = y_hi * 2 + y_lo), z: 4, core: 2. Of those that a mesh axis runs over, the one named last changes fastest.
Arguments:
- assembled: bfloat16 [65536, 1536], P(('grp', 'pan')), may hold values from -6 to 6
- dest_group: int32 [128, 8], P(('grp', 'pan')), may hold values from 0 to 3, as said below
- block_mask: int32 [1024, 24], P(('grp', 'pan')), may hold values 0 or 1
Outputs:
- sign_rows: float32 [65536, 1536], P(('grp', 'pan'))
Inputs may be any that keep to these rules, and one draw needn't show every extreme that they name: `dest_group`: each device's 8 entries name every region equally often.
All inputs are finite; a program needn't handle non-finite values. No bound on the sum of `block_mask` on one device may be relied on, other than what follows from the above.
Results may differ from a plain program's by a relative error of at most 0.0049.
Values may be sent and summed in bfloat16 or wider, within the bound.
A program may use at most 64 MiB of HBM per device.

v0:
```python
import jax
import jax.numpy as jnp
from jax import lax
from jax.sharding import PartitionSpec as P

ITERS = 2


def extended(cells, sides, width):
    for axis, dim in sides:
        count = lax.axis_size(axis)
        head = lax.slice_in_dim(cells, 0, width, axis=dim)
        tail = lax.slice_in_dim(cells, cells.shape[dim] - width, cells.shape[dim], axis=dim)
        cells = jnp.concatenate(
            [
                lax.ppermute(tail, axis, [(i, (i + 1) % count) for i in range(count)]),
                cells,
                lax.ppermute(head, axis, [((i + 1) % count, i) for i in range(count)]),
            ],
            axis=dim,
        )
    return cells


def band_product(factor_one, factor_two):
    tile_rows = factor_one.shape[0]
    padded = extended(factor_two, (("pan", 0),), tile_rows)
    lower_rows = padded[:tile_rows, tile_rows:]
    upper_rows = padded[2 * tile_rows :, : 2 * tile_rows]
    summed = jnp.dot(
        factor_one[:, tile_rows : 2 * tile_rows], factor_two, preferred_element_type=jnp.float32
    )
    summed = summed.at[:, : 2 * tile_rows].add(
        jnp.dot(factor_one[:, :tile_rows], lower_rows, preferred_element_type=jnp.float32)
    )
    summed = summed.at[:, tile_rows:].add(
        jnp.dot(factor_one[:, 2 * tile_rows :], upper_rows, preferred_element_type=jnp.float32)
    )
    return summed


def on_device(assembled, dest_group, block_mask):
    tile_rows = assembled.shape[0]
    band_cols = assembled.shape[1]
    blocks = block_mask.shape[0]
    atom_rows = tile_rows // blocks
    groups = lax.axis_size("grp")
    row_order = jnp.argsort(dest_group[0], stable=True)
    sorted_rows = assembled.reshape(blocks, atom_rows, band_cols)[row_order]
    outgoing = sorted_rows.reshape(groups, blocks // groups * atom_rows, band_cols)
    arrived = lax.all_to_all(outgoing, "grp", split_axis=0, concat_axis=0, tiled=True)
    owned_rows = arrived.reshape(tile_rows, band_cols)
    keep_mask = jnp.broadcast_to(
        block_mask.astype(jnp.float32)[:, None, :, None], (blocks, atom_rows, 3 * blocks, atom_rows)
    )
    keep_mask = keep_mask.reshape(tile_rows, band_cols)
    current = owned_rows * keep_mask.astype(jnp.bfloat16)
    row_index = lax.broadcasted_iota(jnp.int32, (tile_rows, band_cols), 0)
    col_index = lax.broadcasted_iota(jnp.int32, (tile_rows, band_cols), 1)
    identity = (col_index == row_index + tile_rows).astype(jnp.float32)
    result = None
    for sweep in range(ITERS):
        square = keep_mask * band_product(current, current)
        factor = (3.0 * identity - square / (3.0 * tile_rows)).astype(jnp.bfloat16)
        result = 0.5 * keep_mask * band_product(current, factor)
        if sweep + 1 < ITERS:
            current = result.astype(jnp.bfloat16)
    return result


def solution(mesh):
    in_specs = (P(("grp", "pan"), None), P(("grp", "pan"), None), P(("grp", "pan"), None))
    out_specs = P(("grp", "pan"), None)
    return jax.shard_map(
        on_device, mesh=mesh, in_specs=in_specs, out_specs=out_specs, check_vma=False
    )
```

profile of v0, /device:TPU:1, one launch (start us, length us, event | category | flops | bytes accessed | tf_op | source)
XLA Modules:
  0.0 201.2 jit_solution(95354447111489215)
XLA Ops:
  0.0 0.0 copy-start
  0.0 1.7 sort.17
  1.7 0.0 copy-done
  1.8 1.8 gather_fusion
  3.6 0.0 copy-start.2
  3.6 6.1 %all-to-all-start = ((bf16[4,128,1536]{2,1,0:T(8,128)(2,1)}), bf16[4,128,1536]{2,1,0:T(8,128)(2,1)S(1)}, u32[]{:S(2)}, u32[]{:S(2)}) async-start(bf16[4,128,1536]{2,1,0:T(8,128)(2,1)} %bitcast.12), calls=%async_computation | async-start | bytes 3145728 | tf_op jit(solution)/shard_map/all_to_all | solution.py:51
  9.7 0.0 copy-done.2
  9.7 3.1 %broadcast_in_dim.4 = f32[8,64,24,64]{3,2,1,0:T(8,128)} broadcast(f32[8,24]{1,0:T(8,128)S(1)} %convert_element_type.16), dimensions={0,2} | broadcast | bytes 3146496 | tf_op jit(solution)/shard_map/broadcast_in_dim | solution.py:53
  12.8 6.2 %reshape.200 = f32[512,1536]{1,0:T(8,128)} reshape(f32[8,64,24,64]{3,2,1,0:T(8,128)} %broadcast_in_dim.4) | data formatting | bytes 6291456 | tf_op jit(solution)/shard_map/reshape | solution.py:56
  19.0 11.4 %all-to-all-done = bf16[4,128,1536]{2,1,0:T(8,128)(2,1)S(1)} async-done(((bf16[4,128,1536]{2,1,0:T(8,128)(2,1)}), bf16[4,128,1536]{2,1,0:T(8,128)(2,1)S(1)}, u32[]{:S(2)}, u32[]{:S(2)}) %all-to-all-start) | async-done | bytes 1572896 | tf_op jit(solution)/shard_map/all_to_all | solution.py:51
  30.4 2.2 %bitcast_multiply_fusion = bf16[512,1536]{1,0:T(8,128)(2,1)S(1)} fusion(bf16[4,128,1536]{2,1,0:T(8,128)(2,1)S(1)} %all-to-all-done, f32[512,1536]{1,0:T(8,128)} %reshape.200), kind=kLoop, calls=%fused_computation.24 | loop fusion | flops 1572864 | bytes 6291456 | tf_op jit(solution)/shard_map/mul | solution.py:57
  32.6 1.7 collective-permute-start
  34.3 4.5 %collective-permute-start.1 = (bf16[512,1536]{1,0:T(8,128)(2,1)S(1)}, bf16[512,1536]{1,0:T(8,128)(2,1)S(1)}, u32[]{:S(2)}, u32[]{:S(2)}) collective-permute-start(bf16[512,1536]{1,0:T(8,128)(2,1)S(1)} %bitcast_multiply_fusion), channel_id=1, source_target_pairs={{1,0},{2,1},{3,2},{4,3},{5,4},{6,5},{7,6},{8,7},{9,8},{10,9},{11,1... | collective-permute-start | bytes 4718600 | tf_op jit(solution)/shard_map/ppermute | solution.py:18
  38.8 0.7 compare_reduce_fusion
  39.5 1.0 fusion.32
  40.5 32.1 %collective-permute-done = bf16[512,1536]{1,0:T(8,128)(2,1)S(1)} collective-permute-done((bf16[512,1536]{1,0:T(8,128)(2,1)S(1)}, bf16[512,1536]{1,0:T(8,128)(2,1)S(1)}, u32[]{:S(2)}, u32[]{:S(2)}) %collective-permute-start) | collective-permute-done | bytes 1572896 | tf_op jit(solution)/shard_map/ppermute | solution.py:16
  72.6 1.6 fusion.2
  74.2 0.0 copy-start.1
  74.2 0.0 collective-permute-done.1
  74.2 0.8 fusion.9
  75.0 1.1 copy-done.1
  76.1 0.7 fusion
  76.8 0.1 collective-permute-start.2
  76.9 5.7 %collective-permute-start.3 = (bf16[512,1536]{1,0:T(8,128)(2,1)S(1)}, bf16[512,1536]{1,0:T(8,128)(2,1)S(1)}, u32[]{:S(2)}, u32[]{:S(2)}) collective-permute-start(bf16[512,1536]{1,0:T(8,128)(2,1)S(1)} %fusion), channel_id=1, source_target_pairs={{1,0},{2,1},{3,2},{4,3},{5,4},{6,5},{7,6},{8,7},{9,8},{10,9},{11,1... | collective-permute-start | bytes 4718600 | tf_op jit(solution)/shard_map/ppermute | solution.py:18
  82.5 1.0 fusion.30
  83.5 32.0 %collective-permute-done.2 = bf16[512,1536]{1,0:T(8,128)(2,1)S(1)} collective-permute-done((bf16[512,1536]{1,0:T(8,128)(2,1)S(1)}, bf16[512,1536]{1,0:T(8,128)(2,1)S(1)}, u32[]{:S(2)}, u32[]{:S(2)}) %collective-permute-start.2) | collective-permute-done | bytes 1572896 | tf_op jit(solution)/shard_map/ppermute | solution.py:16
  115.5 1.6 fusion.3
  117.1 0.0 collective-permute-done.3
  117.1 0.8 fusion.8
  117.9 0.7 multiply_convert_fusion
  118.6 0.1 collective-permute-start.4
  118.7 5.7 %collective-permute-start.5 = (bf16[512,1536]{1,0:T(8,128)(2,1)S(1)}, bf16[512,1536]{1,0:T(8,128)(2,1)S(1)}, u32[]{:S(2)}, u32[]{:S(2)}) collective-permute-start(bf16[512,1536]{1,0:T(8,128)(2,1)S(1)} %multiply_convert_fusion), channel_id=1, source_target_pairs={{1,0},{2,1},{3,2},{4,3},{5,4},{6,5},{7,6},{8,7},{9,8},{10,9},{11,1... | collective-permute-start | bytes 4718600 | tf_op jit(solution)/shard_map/ppermute | solution.py:18
  124.4 1.0 fusion.24
  125.4 31.1 %collective-permute-done.4 = bf16[512,1536]{1,0:T(8,128)(2,1)S(1)} collective-permute-done((bf16[512,1536]{1,0:T(8,128)(2,1)S(1)}, bf16[512,1536]{1,0:T(8,128)(2,1)S(1)}, u32[]{:S(2)}, u32[]{:S(2)}) %collective-permute-start.4) | collective-permute-done | bytes 1572896 | tf_op jit(solution)/shard_map/ppermute | solution.py:16
  156.4 1.6 fusion.4
  158.0 0.0 collective-permute-done.5
  158.0 0.8 fusion.7
  158.8 0.7 fusion.1
  159.5 0.3 collective-permute-start.6
  159.8 5.7 %collective-permute-start.7 = (bf16[512,1536]{1,0:T(8,128)(2,1)S(1)}, bf16[512,1536]{1,0:T(8,128)(2,1)S(1)}, u32[]{:S(2)}, u32[]{:S(2)}) collective-permute-start(bf16[512,1536]{1,0:T(8,128)(2,1)S(1)} %fusion.1), channel_id=1, source_target_pairs={{1,0},{2,1},{3,2},{4,3},{5,4},{6,5},{7,6},{8,7},{9,8},{10,9},{11,1... | collective-permute-start | bytes 4718600 | tf_op jit(solution)/shard_map/ppermute | solution.py:18
  165.4 1.0 fusion.22
  166.4 30.1 %collective-permute-done.6 = bf16[512,1536]{1,0:T(8,128)(2,1)S(1)} collective-permute-done((bf16[512,1536]{1,0:T(8,128)(2,1)S(1)}, bf16[512,1536]{1,0:T(8,128)(2,1)S(1)}, u32[]{:S(2)}, u32[]{:S(2)}) %collective-permute-start.6) | collective-permute-done | bytes 1572896 | tf_op jit(solution)/shard_map/ppermute | solution.py:16
  196.6 1.6 fusion.5
  198.1 0.0 collective-permute-done.7
  198.2 0.8 fusion.6
  198.9 2.3 %multiply_multiply_fusion = f32[512,1536]{1,0:T(8,128)} fusion(f32[512,1536]{1,0:T(8,128)S(1)} %fusion.6, f32[512,1536]{1,0:T(8,128)S(1)} %copy-done.1), kind=kLoop, calls=%fused_computation.11 | loop fusion | flops 1572864 | bytes 9437184 | tf_op jit(solution)/shard_map/mul | solution.py:65
  (5 shorter events, 0.0 us)
Async XLA Ops:
  0.0 1.8 copy-start
  3.6 6.1 %copy-start.2 = (s32[8,24]{1,0:T(8,128)S(1)}, s32[8,24]{1,0:T(8,128)}, u32[]{:S(2)}) copy-start(s32[8,24]{1,0:T(8,128)} %param.21) | copy-start | bytes 2308
  3.6 26.8 %all-to-all-start = ((bf16[4,128,1536]{2,1,0:T(8,128)(2,1)}), bf16[4,128,1536]{2,1,0:T(8,128)(2,1)S(1)}, u32[]{:S(2)}, u32[]{:S(2)}) async-start(bf16[4,128,1536]{2,1,0:T(8,128)(2,1)} %bitcast.12), calls=%async_computation | async-start | bytes 3145728 | tf_op jit(solution)/shard_map/all_to_all | solution.py:51
  32.6 40.0 %collective-permute-start = (bf16[512,1536]{1,0:T(8,128)(2,1)S(1)}, bf16[512,1536]{1,0:T(8,128)(2,1)S(1)}, u32[]{:S(2)}, u32[]{:S(2)}) collective-permute-start(bf16[512,1536]{1,0:T(8,128)(2,1)S(1)} %bitcast_multiply_fusion), channel_id=1, source_target_pairs={{0,1},{1,2},{2,3},{3,4},{4,5},{5,6},{6,7},{7,8},{8,9},{9,10},{10,1... | collective-permute-start | bytes 4718600 | tf_op jit(solution)/shard_map/ppermute | solution.py:16
  34.3 39.9 %collective-permute-start.1 = (bf16[512,1536]{1,0:T(8,128)(2,1)S(1)}, bf16[512,1536]{1,0:T(8,128)(2,1)S(1)}, u32[]{:S(2)}, u32[]{:S(2)}) collective-permute-start(bf16[512,1536]{1,0:T(8,128)(2,1)S(1)} %bitcast_multiply_fusion), channel_id=1, source_target_pairs={{1,0},{2,1},{3,2},{4,3},{5,4},{6,5},{7,6},{8,7},{9,8},{10,9},{11,1... | collective-permute-start | bytes 4718600 | tf_op jit(solution)/shard_map/ppermute | solution.py:18
  74.2 1.9 copy-start.1
  76.8 38.7 %collective-permute-start.2 = (bf16[512,1536]{1,0:T(8,128)(2,1)S(1)}, bf16[512,1536]{1,0:T(8,128)(2,1)S(1)}, u32[]{:S(2)}, u32[]{:S(2)}) collective-permute-start(bf16[512,1536]{1,0:T(8,128)(2,1)S(1)} %fusion), channel_id=1, source_target_pairs={{0,1},{1,2},{2,3},{3,4},{4,5},{5,6},{6,7},{7,8},{8,9},{9,10},{10,1... | collective-permute-start | bytes 4718600 | tf_op jit(solution)/shard_map/ppermute | solution.py:16
  76.9 40.2 %collective-permute-start.3 = (bf16[512,1536]{1,0:T(8,128)(2,1)S(1)}, bf16[512,1536]{1,0:T(8,128)(2,1)S(1)}, u32[]{:S(2)}, u32[]{:S(2)}) collective-permute-start(bf16[512,1536]{1,0:T(8,128)(2,1)S(1)} %fusion), channel_id=1, source_target_pairs={{1,0},{2,1},{3,2},{4,3},{5,4},{6,5},{7,6},{8,7},{9,8},{10,9},{11,1... | collective-permute-start | bytes 4718600 | tf_op jit(solution)/shard_map/ppermute | solution.py:18
  118.6 37.8 %collective-permute-start.4 = (bf16[512,1536]{1,0:T(8,128)(2,1)S(1)}, bf16[512,1536]{1,0:T(8,128)(2,1)S(1)}, u32[]{:S(2)}, u32[]{:S(2)}) collective-permute-start(bf16[512,1536]{1,0:T(8,128)(2,1)S(1)} %multiply_convert_fusion), channel_id=1, source_target_pairs={{0,1},{1,2},{2,3},{3,4},{4,5},{5,6},{6,7},{7,8},{8,9},{9,10},{10,1... | collective-permute-start | bytes 4718600 | tf_op jit(solution)/shard_map/ppermute | solution.py:16
  118.7 39.3 %collective-permute-start.5 = (bf16[512,1536]{1,0:T(8,128)(2,1)S(1)}, bf16[512,1536]{1,0:T(8,128)(2,1)S(1)}, u32[]{:S(2)}, u32[]{:S(2)}) collective-permute-start(bf16[512,1536]{1,0:T(8,128)(2,1)S(1)} %multiply_convert_fusion), channel_id=1, source_target_pairs={{1,0},{2,1},{3,2},{4,3},{5,4},{6,5},{7,6},{8,7},{9,8},{10,9},{11,1... | collective-permute-start | bytes 4718600 | tf_op jit(solution)/shard_map/ppermute | solution.py:18
  159.5 37.1 %collective-permute-start.6 = (bf16[512,1536]{1,0:T(8,128)(2,1)S(1)}, bf16[512,1536]{1,0:T(8,128)(2,1)S(1)}, u32[]{:S(2)}, u32[]{:S(2)}) collective-permute-start(bf16[512,1536]{1,0:T(8,128)(2,1)S(1)} %fusion.1), channel_id=1, source_target_pairs={{0,1},{1,2},{2,3},{3,4},{4,5},{5,6},{6,7},{7,8},{8,9},{9,10},{10,1... | collective-permute-start | bytes 4718600 | tf_op jit(solution)/shard_map/ppermute | solution.py:16
  159.8 38.4 %collective-permute-start.7 = (bf16[512,1536]{1,0:T(8,128)(2,1)S(1)}, bf16[512,1536]{1,0:T(8,128)(2,1)S(1)}, u32[]{:S(2)}, u32[]{:S(2)}) collective-permute-start(bf16[512,1536]{1,0:T(8,128)(2,1)S(1)} %fusion.1), channel_id=1, source_target_pairs={{1,0},{2,1},{3,2},{4,3},{5,4},{6,5},{7,6},{8,7},{9,8},{10,9},{11,1... | collective-permute-start | bytes 4718600 | tf_op jit(solution)/shard_map/ppermute | solution.py:18
where the time goes:
time: 204 us; the launch traced here: 201 us
  waiting for transfers between devices  137 us (67%)
  starting transfers between devices  29.7 us (15%)
  matrix products  13.3 us (7%)
  local copies, waits for them, and re-layouts  12.2 us (6%)
  other arithmetic  9.07 us (4%)
    ppermute x4, waiting for transfers between devices, extended(): lax.ppermute(tail, axis, [(i, (i + 1) % count) for i in range(count)])  125 us
    ppermute x4, starting transfers between devices, extended(): lax.ppermute(head, axis, [((i + 1) % count, i) for i in range(count)])  21.5 us
    all_to_all x1, waiting for transfers between devices, on_device(): lax.all_to_all(outgoing, 'grp', split_axis=0, concat_axis=0, tiled=True)  11.4 us
    dot_general x4, matrix products, band_product(): jnp.dot(factor_one[:, :tile_rows], lower_rows, preferred_element_type=jnp...  6.31 us
    reshape x1, local copies, waits for them, and re-layouts, on_device(): keep_mask = keep_mask.reshape(tile_rows, band_cols)  6.17 us
    all_to_all x1, starting transfers between devices, on_device(): lax.all_to_all(outgoing, 'grp', split_axis=0, concat_axis=0, tiled=True)  6.1 us
  transfers between devices with their start and end apart: 9, of which 5 were waited for; matrix products, arithmetic and copies ran while one was open for 10% of the time, Pallas kernels for 0%

commit v1 on v0

v1 whole, which is shorter than its diff:
```python
import jax
import jax.numpy as jnp
from jax import lax
from jax.experimental import pallas as pl
from jax.experimental.pallas import tpu as pltpu
from jax.sharding import PartitionSpec as P

MESH = pl.DeviceIdType.MESH
ATOM = 64
CB = 8
T = ATOM * CB
CHUNK = 2 * ATOM
H = 256
BF = jnp.bfloat16
F32 = jnp.float32


def kernel(
    x_ref, dest_ref, mask_ref, out_ref,
    srt, land, mine, mask_l, mask_r, keep, keep_um, keep_lp,
    a_row, a_hl, a_hr, f_row, f_um, f_lp, f_dm, f_dp,
    b_row, b_hl, b_hr, h_row, h_um, h_lp, h_dm, h_dp,
    go_s, go_r, halo_s, halo_r, tile_s, tile_r, m_s, m_r,
):
    g = lax.axis_index("grp")
    p = lax.axis_index("pan")
    n = lax.axis_size("pan")
    core = lax.rem(g, 2)
    sib = g + 1 - 2 * core
    far = lax.rem(g + 2, 4)
    far_sib = lax.rem(sib + 2, 4)
    partners = (g, sib, far, far_sib)
    left = (g, lax.rem(p + n - 1, n))
    right = (g, lax.rem(p + 1, n))

    barrier = pltpu.get_barrier_semaphore()
    for other in partners[1:]:
        pl.semaphore_signal(barrier, inc=1, device_id=(other, p), device_id_type=MESH)
    for other in (left, right):
        pl.semaphore_signal(barrier, inc=1, device_id=other, device_id_type=MESH)

    def one_hot(rows, cols, of_row, of_col):
        row = of_row(lax.broadcasted_iota(jnp.int32, (rows, cols), 0))
        return (row == of_col(lax.broadcasted_iota(jnp.int32, (rows, cols), 1))).astype(F32)

    eye = one_hot(CB, CB, lambda v: v, lambda v: v)
    lane = lax.broadcasted_iota(jnp.int32, (1, CB), 1)
    key_row = (dest_ref[...] * CB + lane).astype(F32)
    key_col = jnp.sum(eye * key_row, axis=1, keepdims=True)
    rank = jnp.sum((key_col < key_row).astype(F32), axis=0, keepdims=True)
    spread = one_hot(CB, T, lambda v: v, lambda v: v // ATOM)
    slot = jnp.sum(spread * jnp.sum(eye * rank, axis=1, keepdims=True), axis=0, keepdims=True)
    slot = slot * ATOM + (lax.broadcasted_iota(jnp.int32, (1, T), 1) % ATOM).astype(F32)

    def gather(r):
        want = (partners[r] * CHUNK + lax.broadcasted_iota(jnp.int32, (CHUNK, T), 0)).astype(F32)
        pick = (want == slot).astype(BF)
        srt[r] = jnp.dot(pick, x_ref[...], preferred_element_type=F32).astype(BF)

    for r in (2, 3, 1, 0):
        gather(r)
    mine[...] = jnp.zeros_like(mine)
    mine[:, : 3 * CB] = mask_ref[...].astype(F32)
    pl.semaphore_wait(barrier, 5)

    def remote(src, dst, ss, rs, to):
        copy = pltpu.make_async_remote_copy(
            src_ref=src, dst_ref=dst, send_sem=ss, recv_sem=rs, device_id=to, device_id_type=MESH
        )
        copy.start()
        return copy

    pending = []
    arrive = {}
    my_rows = pl.multiple_of(g * CHUNK, CHUNK)
    for t in range(2):
        for r in (2, 3, 1):
            copy = remote(
                srt.at[r, pl.ds(t * ATOM, ATOM)],
                land.at[pl.ds(pl.multiple_of(my_rows + t * ATOM, ATOM), ATOM)],
                go_s.at[r, t], go_r.at[r, t], (partners[r], p),
            )
            arrive[r, t] = copy
    pending.append(remote(mine, mask_l, m_s.at[0], m_r.at[0], right))
    pending.append(remote(mine, mask_r, m_s.at[1], m_r.at[1], left))

    def expand(block, dst):
        rows = block.shape[0] * ATOM
        cols = block.shape[1] * ATOM
        up = (lax.broadcasted_iota(jnp.int32, (rows, CB), 0) // ATOM) == lax.broadcasted_iota(jnp.int32, (rows, CB), 1)
        across = lax.broadcasted_iota(jnp.int32, (block.shape[1], cols), 0) == (
            lax.broadcasted_iota(jnp.int32, (block.shape[1], cols), 1) // ATOM
        )
        tall = jnp.dot(up.astype(BF), block.astype(BF), preferred_element_type=F32)
        dst[...] = jnp.dot(tall.astype(BF), across.astype(BF), preferred_element_type=F32).astype(BF)

    expand(mine[:, : 3 * CB], keep)

    halo = {}

    def place(r, t):
        rows = pl.ds(pl.multiple_of(partners[r] * CHUNK + t * ATOM, ATOM), ATOM)
        if r == 0:
            a_row[rows, :] = srt[0, t * ATOM : (t + 1) * ATOM, :] * keep[rows, :]
        else:
            arrive[r, t].wait_recv()
            a_row[rows, :] = land[rows, :] * keep[rows, :]
        halo[0, r, t] = remote(
            a_row.at[rows, pl.ds(T, 2 * T)], a_hl.at[rows], halo_s.at[0, r, t], halo_r.at[0, r, t], right
        )
        halo[1, r, t] = remote(
            a_row.at[rows, pl.ds(0, 2 * T)], a_hr.at[rows], halo_s.at[1, r, t], halo_r.at[1, r, t], left
        )

    order = ((0, 0), (0, 1), (1, 0), (1, 1), (2, 0), (3, 0), (2, 1), (3, 1))
    for r, t in order:
        place(r, t)

    pending[0].wait_recv()
    pending[1].wait_recv()
    expand(mask_l[:, 2 * CB : 3 * CB], keep_um)
    expand(mask_r[:, :CB], keep_lp)
    for r, t in order:
        for side in (0, 1):
            halo[side, r, t].wait_recv()

    def tile_of(ref, k):
        return ref.at[:, pl.ds(k * T, T)]

    def product(pairs, finish):
        for i in range(T // H):
            for j in range(T // H):
                acc = None
                for a, b in pairs:
                    part = jnp.dot(
                        a[i * H : (i + 1) * H, :], b[:, j * H : (j + 1) * H], preferred_element_type=F32
                    )
                    acc = part if acc is None else acc + part
                finish(i, j, acc)

    def to_factor(dst, mask, diagonal):
        def finish(i, j, acc):
            at = (slice(i * H, (i + 1) * H), slice(j * H, (j + 1) * H))
            value = acc * mask[at].astype(F32) * (-1.0 / (3.0 * T))
            if diagonal and i == j:
                same = lax.broadcasted_iota(jnp.int32, (H, H), 0) == lax.broadcasted_iota(jnp.int32, (H, H), 1)
                value = jnp.where(same, 3.0 + value, value)
            dst[at] = value.astype(BF)

        return finish

    def to_next(dst, mask, dtype):
        def finish(i, j, acc):
            at = (slice(i * H, (i + 1) * H), slice(j * H, (j + 1) * H))
            dst[at] = (0.5 * acc * mask[at].astype(F32)).astype(dtype)

        return finish

    k_l, k_d, k_u = (tile_of(keep, k) for k in range(3))

    def tiles(row, um_ref, lp_ref, dm_ref, dp_ref):
        return dict(l=tile_of(row, 0), d=tile_of(row, 1), u=tile_of(row, 2), um=um_ref, lp=lp_ref, dm=dm_ref, dp=dp_ref)

    a = tiles(a_row, tile_of(a_hl, 1), tile_of(a_hr, 0), tile_of(a_hl, 0), tile_of(a_hr, 1))
    b = tiles(b_row, tile_of(b_hl, 1), tile_of(b_hr, 0), tile_of(b_hl, 0), tile_of(b_hr, 1))
    f = tiles(f_row, f_um, f_lp, f_dm, f_dp)
    h = tiles(h_row, h_um, h_lp, h_dm, h_dp)

    def swap(k, src, dst_from_left, dst_from_right):
        return (
            remote(src, dst_from_left, tile_s.at[k, 0], tile_r.at[k, 0], right),
            remote(src, dst_from_right, tile_s.at[k, 1], tile_r.at[k, 1], left),
        )

    def node(x, y):
        return [(x["d"], y["d"]), (x["u"], y["lp"]), (x["l"], y["um"])]

    def edge_um(x, y):
        return [(x["dm"], y["um"]), (x["um"], y["d"])]

    def edge_lp(x, y):
        return [(x["dp"], y["lp"]), (x["lp"], y["d"])]

    def edge_l(x, y):
        return [(x["d"], y["l"]), (x["l"], y["dm"])]

    def edge_u(x, y):
        return [(x["d"], y["u"]), (x["u"], y["dp"])]

    product(node(a, a), to_factor(f["d"], k_d, True))
    sent_f = swap(0, f["d"], f_dm, f_dp)
    product(edge_um(a, a), to_factor(f["um"], keep_um, False))
    product(edge_lp(a, a), to_factor(f["lp"], keep_lp, False))
    product(node(a, f), to_next(b["d"], k_d, BF))
    sent_b = swap(1, b["d"], b["dm"], b["dp"])
    product(edge_l(a, a), to_factor(f["l"], k_l, False))
    product(edge_u(a, a), to_factor(f["u"], k_u, False))
    product(edge_um(a, f), to_next(b["um"], keep_um, BF))
    product(edge_lp(a, f), to_next(b["lp"], keep_lp, BF))

    sent_f[0].wait_recv()
    product(edge_l(a, f), to_next(b["l"], k_l, BF))
    sent_f[1].wait_recv()
    product(edge_u(a, f), to_next(b["u"], k_u, BF))

    product(node(b, b), to_factor(h["d"], k_d, True))
    sent_h = swap(2, h["d"], h_dm, h_dp)
    sent_b[0].wait_recv()
    product(edge_um(b, b), to_factor(h["um"], keep_um, False))
    product(edge_l(b, b), to_factor(h["l"], k_l, False))
    sent_b[1].wait_recv()
    product(edge_lp(b, b), to_factor(h["lp"], keep_lp, False))
    product(edge_u(b, b), to_factor(h["u"], k_u, False))
    product(node(b, h), to_next(out_ref.at[:, pl.ds(T, T)], k_d, F32))
    sent_h[0].wait_recv()
    product(edge_l(b, h), to_next(out_ref.at[:, pl.ds(0, T)], k_l, F32))
    sent_h[1].wait_recv()
    product(edge_u(b, h), to_next(out_ref.at[:, pl.ds(2 * T, T)], k_u, F32))

    for copy in arrive.values():
        copy.wait_send()
    for copy in halo.values():
        copy.wait_send()
    for copy in (*pending, *sent_f, *sent_b, *sent_h):
        copy.wait_send()


def on_device(assembled, dest_group, block_mask):
    tile = pltpu.VMEM((T, T), BF)
    row = pltpu.VMEM((T, 3 * T), BF)
    pair = pltpu.VMEM((T, 2 * T), BF)
    dma = pltpu.SemaphoreType.DMA
    return pl.pallas_call(
        kernel,
        out_shape=jax.ShapeDtypeStruct((T, 3 * T), F32),
        in_specs=[
            pl.BlockSpec(memory_space=pltpu.VMEM),
            pl.BlockSpec(memory_space=pltpu.VMEM),
            pl.BlockSpec(memory_space=pltpu.VMEM),
        ],
        out_specs=pl.BlockSpec(memory_space=pltpu.VMEM),
        scratch_shapes=[
            pltpu.VMEM((4, CHUNK, 3 * T), BF), row,
            pltpu.VMEM((CB, 128), F32), pltpu.VMEM((CB, 128), F32), pltpu.VMEM((CB, 128), F32),
            row, tile, tile,
            row, pair, pair, row, tile, tile, tile, tile,
            row, pair, pair, row, tile, tile, tile, tile,
            dma((4, 2)), dma((4, 2)), dma((2, 4, 2)), dma((2, 4, 2)), dma((3, 2)), dma((3, 2)), dma((2,)), dma((2,)),
        ],
        compiler_params=pltpu.CompilerParams(
            collective_id=0, has_side_effects=True, vmem_limit_bytes=56 * 2**20
        ),
        cost_estimate=pl.CostEstimate(flops=40 * 2 * T**3, bytes_accessed=9 * T * T * 2, transcendentals=0),
        name="sign_steps",
    )(assembled, dest_group, block_mask)


def solution(mesh):
    spec = P(("grp", "pan"), None)
    return jax.shard_map(on_device, mesh=mesh, in_specs=(spec, spec, spec), out_specs=spec, check_vma=False)
```

time: 204 us -> 104 us (0.51); the launches traced: 201 us -> 103 us
  waiting for transfers between devices: 137 us -> 0 us
  Pallas kernels: 0 us -> 99.6 us
  starting transfers between devices: 29.7 us -> 0 us
  matrix products: 13.3 us -> 0 us
  other arithmetic: 9.07 us -> 0 us
  local copies, waits for them, and re-layouts: 12.2 us -> 3.76 us
    ppermute x8 -> x0, waiting for transfers between devices: 125 us -> none  [the longest x4 125 us: extended(): lax.ppermute(tail, axis, [(i, (i + 1) % count) for i in range(count)])]
    pallas_call x0 -> x1, Pallas kernels: none -> 99.6 us  [on_device(): pl.pallas_call(kernel, out_shape=jax.ShapeDtypeStruct((T, 3 * T), F32), i...]
    ppermute x8 -> x0, starting transfers between devices: 23.6 us -> none  [the longest x4 21.5 us: extended(): lax.ppermute(head, axis, [((i + 1) % count, i) for i in range(count)])]
    dot_general x12 -> x0, matrix products: 13.3 us -> none  [the longest x4 6.31 us: band_product(): jnp.dot(factor_one[:, :tile_rows], lower_rows, preferred_element_type=jnp...]
    all_to_all x1 -> x0, waiting for transfers between devices: 11.4 us -> none  [on_device(): lax.all_to_all(outgoing, 'grp', split_axis=0, concat_axis=0, tiled=True)]
    reshape x1 -> x0, local copies, waits for them, and re-layouts: 6.17 us -> none  [on_device(): keep_mask = keep_mask.reshape(tile_rows, band_cols)]
    all_to_all x1 -> x0, starting transfers between devices: 6.1 us -> none  [on_device(): lax.all_to_all(outgoing, 'grp', split_axis=0, concat_axis=0, tiled=True)]
    mul x2 -> x0, other arithmetic: 4.49 us -> none  [the longest x1 2.29 us: on_device(): result = 0.5 * keep_mask * band_product(current, factor)]
  transfers between devices with their start and end apart: 9 -> 0, of which waited for: 5 -> 0; matrix products, arithmetic and copies ran while one was open for 10% -> 0% of each run, Pallas kernels for 0% -> 0%
where the time goes in v1:
time: 104 us; the launch traced here: 103 us
  Pallas kernels  99.6 us (96%)
  local copies, waits for them, and re-layouts  3.76 us (4%)
    pallas_call x1, Pallas kernels, on_device(): pl.pallas_call(kernel, out_shape=jax.ShapeDtypeStruct((T, 3 * T), F32), i...  99.6 us
    unnamed x1, local copies, waits for them, and re-layouts  3.76 us

profile of v1, /device:TPU:1, one launch (start us, length us, event | category | flops | bytes accessed | tf_op | source)
XLA Modules:
  0.0 103.3 jit_solution(15662367430470143371)
XLA Ops:
  0.0 99.6 %sign_steps.1 = f32[512,1536]{1,0:T(8,128)} custom-call(bf16[512,1536]{1,0:T(8,128)(2,1)} %x_ref.1, s32[1,8]{1,0:T(1,128)} %dest_ref.1, s32[8,24]{1,0:T(8,128)} %mask_ref.1), custom_call_target="tpu_custom_call" | custom-call | flops 10737418240 | bytes 4718592 | tf_op jit(solution)/shard_map/sign_steps/pallas_call | solution.py:233
  99.6 3.8 %copy.5 = f32[512,1536]{1,0:T(8,128)} copy(f32[512,1536]{1,0:T(8,128)} %sign_steps.1) | data formatting | bytes 6291456

commit v2 on v1

--- a/solution.py
+++ b/solution.py
@@ -17,27 +17,49 @@
 
 def kernel(
     x_ref, dest_ref, mask_ref, out_ref,
-    srt, land, mine, mask_l, mask_r, keep, keep_um, keep_lp,
+    for_far, for_sib, transit, land, mine, mask_l, mask_r, keep, keep_hl, keep_hr,
     a_row, a_hl, a_hr, f_row, f_um, f_lp, f_dm, f_dp,
     b_row, b_hl, b_hr, h_row, h_um, h_lp, h_dm, h_dp,
-    go_s, go_r, halo_s, halo_r, tile_s, tile_r, m_s, m_r,
+    sib_s, sib_r, hop_s, hop_r, far_s, far_r, halo_s, halo_r, extra_s, tile_s, tile_r, m_s, m_r,
 ):
     g = lax.axis_index("grp")
     p = lax.axis_index("pan")
     n = lax.axis_size("pan")
     core = lax.rem(g, 2)
+    y_hi = g // 2
+    z = lax.rem(p, 4)
     sib = g + 1 - 2 * core
     far = lax.rem(g + 2, 4)
     far_sib = lax.rem(sib + 2, 4)
-    partners = (g, sib, far, far_sib)
-    left = (g, lax.rem(p + n - 1, n))
-    right = (g, lax.rem(p + 1, n))
+    wraps = jnp.logical_or(z == 0, z == 3)
+
+    def across(pan):
+        return pan + 4 - 8 * lax.rem(pan // 4, 2)
+
+    before, after = lax.rem(p + n - 1, n), lax.rem(p + 1, n)
+    inner = across(p)
+    left, right = (g, before), (g, after)
+    outer_to = (far, inner)
+    inner_to = ((g, inner), (sib, inner))
+    chunk_of = (g, sib, far, far_sib)
 
     barrier = pltpu.get_barrier_semaphore()
-    for other in partners[1:]:
-        pl.semaphore_signal(barrier, inc=1, device_id=(other, p), device_id_type=MESH)
-    for other in (left, right):
+
+    def greet(other):
         pl.semaphore_signal(barrier, inc=1, device_id=other, device_id_type=MESH)
+
+    for other in ((sib, p), outer_to, *inner_to, left, right):
+        greet(other)
+
+    @pl.when(z == 0)
+    def _():
+        for who in (g, sib):
+            greet((who, across(before)))
+
+    @pl.when(z == 3)
+    def _():
+        for who in (g, sib):
+            greet((who, across(after)))
 
     def one_hot(rows, cols, of_row, of_col):
         row = of_row(lax.broadcasted_iota(jnp.int32, (rows, cols), 0))
@@ -52,77 +74,129 @@
     slot = jnp.sum(spread * jnp.sum(eye * rank, axis=1, keepdims=True), axis=0, keepdims=True)
     slot = slot * ATOM + (lax.broadcasted_iota(jnp.int32, (1, T), 1) % ATOM).astype(F32)
 
-    def gather(r):
-        want = (partners[r] * CHUNK + lax.broadcasted_iota(jnp.int32, (CHUNK, T), 0)).astype(F32)
+    def rows_for(group):
+        want = (group * CHUNK + lax.broadcasted_iota(jnp.int32, (CHUNK, T), 0)).astype(F32)
         pick = (want == slot).astype(BF)
-        srt[r] = jnp.dot(pick, x_ref[...], preferred_element_type=F32).astype(BF)
-
-    for r in (2, 3, 1, 0):
-        gather(r)
+        return jnp.dot(pick, x_ref[...], preferred_element_type=F32).astype(BF)
+
+    def rows_at(k, t, count):
+        return pl.ds(pl.multiple_of(chunk_of[k] * CHUNK + t * ATOM, ATOM), count)
+
+    for_far[0] = rows_for(far)
+    for_far[1] = rows_for(far_sib)
+    for_sib[...] = rows_for(sib)
+    land[rows_at(0, 0, CHUNK), :] = rows_for(g)
     mine[...] = jnp.zeros_like(mine)
     mine[:, : 3 * CB] = mask_ref[...].astype(F32)
-    pl.semaphore_wait(barrier, 5)
-
-    def remote(src, dst, ss, rs, to):
-        copy = pltpu.make_async_remote_copy(
+
+    @pl.when(wraps)
+    def _():
+        pl.semaphore_wait(barrier, 8)
+
+    @pl.when(jnp.logical_not(wraps))
+    def _():
+        pl.semaphore_wait(barrier, 6)
+
+    def describe(src, dst, ss, rs, to):
+        return pltpu.make_async_remote_copy(
             src_ref=src, dst_ref=dst, send_sem=ss, recv_sem=rs, device_id=to, device_id_type=MESH
         )
+
+    pending = []
+
+    def remote(*what):
+        copy = describe(*what)
         copy.start()
+        pending.append((None, copy))
         return copy
 
-    pending = []
+    def remote_when(cond, *what):
+        copy = describe(*what)
+
+        @pl.when(cond)
+        def _():
+            copy.start()
+
+        pending.append((cond, copy))
+        return copy
+
+    hop = {}
+    for t in range(2):
+        for k in range(2):
+            rows = pl.ds(t * ATOM, ATOM)
+            hop[k, t] = remote(for_far.at[k, rows], transit.at[k, rows], hop_s.at[k, t], hop_r.at[k, t], outer_to)
+    here = rows_at(0, 0, CHUNK)
+    from_sib = remote(for_sib, land.at[here], sib_s, sib_r, (sib, p))
+    mask_in = (
+        remote(mine, mask_l, m_s.at[0], m_r.at[0], right),
+        remote(mine, mask_r, m_s.at[1], m_r.at[1], left),
+    )
+    halo = []
+    right_cols, left_cols = pl.ds(T, 2 * T), pl.ds(0, 2 * T)
+
+    def spread_out(k, t, count):
+        rows = rows_at(k, t, count)
+        to_right = (land.at[rows, right_cols], a_hl.at[rows], halo_s.at[0, k, t], halo_r.at[0, k, t], right)
+        to_left = (land.at[rows, left_cols], a_hr.at[rows], halo_s.at[1, k, t], halo_r.at[1, k, t], left)
+        if k < 2:
+            halo.append(remote(*to_right))
+            halo.append(remote(*to_left))
+        else:
+            halo.append(remote_when(z != 3, *to_right))
+            halo.append(remote_when(z != 0, *to_left))
+
     arrive = {}
-    my_rows = pl.multiple_of(g * CHUNK, CHUNK)
-    for t in range(2):
-        for r in (2, 3, 1):
-            copy = remote(
-                srt.at[r, pl.ds(t * ATOM, ATOM)],
-                land.at[pl.ds(pl.multiple_of(my_rows + t * ATOM, ATOM), ATOM)],
-                go_s.at[r, t], go_r.at[r, t], (partners[r], p),
-            )
-            arrive[r, t] = copy
-    pending.append(remote(mine, mask_l, m_s.at[0], m_r.at[0], right))
-    pending.append(remote(mine, mask_r, m_s.at[1], m_r.at[1], left))
+
+    def forward(k, t):
+        hop[k, t].wait_recv()
+        rows = pl.ds(t * ATOM, ATOM)
+        at = pl.ds(pl.multiple_of(far * CHUNK + t * ATOM, ATOM), ATOM)
+        who = (g, sib)[k]
+        arrive[k, t] = remote(transit.at[k, rows], land.at[at], far_s.at[k, t], far_r.at[k, t], inner_to[k])
+        remote_when(
+            z == 3, transit.at[k, rows, right_cols], a_hl.at[at], extra_s.at[0, k, t], halo_r.at[0, 2 + k, t],
+            (who, lax.rem(inner + 1, n)),
+        )
+        remote_when(
+            z == 0, transit.at[k, rows, left_cols], a_hr.at[at], extra_s.at[1, k, t], halo_r.at[1, 2 + k, t],
+            (who, lax.rem(inner + n - 1, n)),
+        )
+
+    def settle(k, t):
+        arrive[k, t].wait_recv()
+        spread_out(2 + k, t, ATOM)
 
     def expand(block, dst):
         rows = block.shape[0] * ATOM
         cols = block.shape[1] * ATOM
-        up = (lax.broadcasted_iota(jnp.int32, (rows, CB), 0) // ATOM) == lax.broadcasted_iota(jnp.int32, (rows, CB), 1)
-        across = lax.broadcasted_iota(jnp.int32, (block.shape[1], cols), 0) == (
-            lax.broadcasted_iota(jnp.int32, (block.shape[1], cols), 1) // ATOM
-        )
-        tall = jnp.dot(up.astype(BF), block.astype(BF), preferred_element_type=F32)
-        dst[...] = jnp.dot(tall.astype(BF), across.astype(BF), preferred_element_type=F32).astype(BF)
-
+        up = one_hot(rows, CB, lambda v: v // ATOM, lambda v: v).astype(BF)
+        over = one_hot(block.shape[1], cols, lambda v: v, lambda v: v // ATOM).astype(BF)
+        tall = jnp.dot(up, block.astype(BF), preferred_element_type=F32)
+        dst[...] = jnp.dot(tall.astype(BF), over, preferred_element_type=F32).astype(BF)
+
+    spread_out(0, 0, CHUNK)
+    from_sib.wait_recv()
+    spread_out(1, 0, CHUNK)
     expand(mine[:, : 3 * CB], keep)
-
-    halo = {}
-
-    def place(r, t):
-        rows = pl.ds(pl.multiple_of(partners[r] * CHUNK + t * ATOM, ATOM), ATOM)
-        if r == 0:
-            a_row[rows, :] = srt[0, t * ATOM : (t + 1) * ATOM, :] * keep[rows, :]
-        else:
-            arrive[r, t].wait_recv()
-            a_row[rows, :] = land[rows, :] * keep[rows, :]
-        halo[0, r, t] = remote(
-            a_row.at[rows, pl.ds(T, 2 * T)], a_hl.at[rows], halo_s.at[0, r, t], halo_r.at[0, r, t], right
-        )
-        halo[1, r, t] = remote(
-            a_row.at[rows, pl.ds(0, 2 * T)], a_hr.at[rows], halo_s.at[1, r, t], halo_r.at[1, r, t], left
-        )
-
-    order = ((0, 0), (0, 1), (1, 0), (1, 1), (2, 0), (3, 0), (2, 1), (3, 1))
-    for r, t in order:
-        place(r, t)
-
-    pending[0].wait_recv()
-    pending[1].wait_recv()
-    expand(mask_l[:, 2 * CB : 3 * CB], keep_um)
-    expand(mask_r[:, :CB], keep_lp)
-    for r, t in order:
-        for side in (0, 1):
-            halo[side, r, t].wait_recv()
+    forward(0, 0)
+    forward(1, 0)
+    settle(0, 0)
+    forward(0, 1)
+    settle(1, 0)
+    forward(1, 1)
+    mask_in[0].wait_recv()
+    mask_in[1].wait_recv()
+    expand(mask_l[:, CB : 3 * CB], keep_hl)
+    expand(mask_r[:, : 2 * CB], keep_hr)
+    settle(0, 1)
+    settle(1, 1)
+    a_row[...] = land[...] * keep[...]
+    for copy in halo:
+        copy.wait_recv()
+    a_hl[...] = a_hl[...] * keep_hl[...]
+    a_hr[...] = a_hr[...] * keep_hr[...]
+    keep_um = keep_hl.at[:, pl.ds(T, T)]
+    keep_lp = keep_hr.at[:, pl.ds(0, T)]
 
     def tile_of(ref, k):
         return ref.at[:, pl.ds(k * T, T)]
@@ -217,12 +291,11 @@
     sent_h[1].wait_recv()
     product(edge_u(b, h), to_next(out_ref.at[:, pl.ds(2 * T, T)], k_u, F32))
 
-    for copy in arrive.values():
-        copy.wait_send()
-    for copy in halo.values():
-        copy.wait_send()
-    for copy in (*pending, *sent_f, *sent_b, *sent_h):
-        copy.wait_send()
+    for cond, copy in pending:
+        if cond is None:
+            copy.wait_send()
+        else:
+            pl.when(cond)(copy.wait_send)
 
 
 def on_device(assembled, dest_group, block_mask):
@@ -240,12 +313,13 @@
         ],
         out_specs=pl.BlockSpec(memory_space=pltpu.VMEM),
         scratch_shapes=[
-            pltpu.VMEM((4, CHUNK, 3 * T), BF), row,
+            pltpu.VMEM((2, CHUNK, 3 * T), BF), pltpu.VMEM((CHUNK, 3 * T), BF), pltpu.VMEM((2, CHUNK, 3 * T), BF), row,
             pltpu.VMEM((CB, 128), F32), pltpu.VMEM((CB, 128), F32), pltpu.VMEM((CB, 128), F32),
-            row, tile, tile,
+            row, pair, pair,
             row, pair, pair, row, tile, tile, tile, tile,
             row, pair, pair, row, tile, tile, tile, tile,
-            dma((4, 2)), dma((4, 2)), dma((2, 4, 2)), dma((2, 4, 2)), dma((3, 2)), dma((3, 2)), dma((2,)), dma((2,)),
+            dma, dma, dma((2, 2)), dma((2, 2)), dma((2, 2)), dma((2, 2)),
+            dma((2, 4, 2)), dma((2, 4, 2)), dma((2, 2, 2)), dma((3, 2)), dma((3, 2)), dma((2,)), dma((2,)),
         ],
         compiler_params=pltpu.CompilerParams(
             collective_id=0, has_side_effects=True, vmem_limit_bytes=56 * 2**20

time: 104 us -> 86.5 us (0.83)
  Pallas kernels: 99.6 us -> 82.4 us
    pallas_call x1, Pallas kernels: 99.6 us -> 82.4 us  [on_device(): pl.pallas_call(kernel, out_shape=jax.ShapeDtypeStruct((T, 3 * T), F32), i...]
where the time goes in v2:
time: 86.5 us; the launch traced here: 86.2 us
  Pallas kernels  82.4 us (95%)
  local copies, waits for them, and re-layouts  3.76 us (4%)
    pallas_call x1, Pallas kernels, on_device(): pl.pallas_call(kernel, out_shape=jax.ShapeDtypeStruct((T, 3 * T), F32), i...  82.4 us
    unnamed x1, local copies, waits for them, and re-layouts  3.76 us

profile of v2, /device:TPU:1, one launch (start us, length us, event | category | flops | bytes accessed | tf_op | source)
XLA Modules:
  0.0 86.2 jit_solution(14594437440697056100)
XLA Ops:
  0.0 82.4 %sign_steps.1 = f32[512,1536]{1,0:T(8,128)} custom-call(bf16[512,1536]{1,0:T(8,128)(2,1)} %x_ref.1, s32[1,8]{1,0:T(1,128)} %dest_ref.1, s32[8,24]{1,0:T(8,128)} %mask_ref.1), custom_call_target="tpu_custom_call" | custom-call | flops 10737418240 | bytes 4718592 | tf_op jit(solution)/shard_map/sign_steps/pallas_call | solution.py:306
  82.4 3.8 %copy.5 = f32[512,1536]{1,0:T(8,128)} copy(f32[512,1536]{1,0:T(8,128)} %sign_steps.1) | data formatting | bytes 6291456

commit v3 on v2

v3 whole, which is shorter than its diff:
```python
import functools

import jax
import jax.numpy as jnp
from jax import lax
from jax.experimental import pallas as pl
from jax.experimental.pallas import tpu as pltpu
from jax.sharding import PartitionSpec as P

MESH = pl.DeviceIdType.MESH
ATOM = 64
CB = 8
T = ATOM * CB
CHUNK = 2 * ATOM
H = 256
CUTS = (0, 64, 96, 128)
PIECES = len(CUTS) - 1
BF = jnp.bfloat16
F32 = jnp.float32


def kernel(
    x_ref, dest_ref, mask_ref, out_ref,
    for_far, for_sib, transit, land, mine, mask_l, mask_r, keep, keep_hl, keep_hr,
    a_row, a_hl, a_hr, f_row, f_um, f_lp, f_dm, f_dp,
    b_row, b_hl, b_hr, h_row, h_um, h_lp, h_dm, h_dp,
    sib_s, sib_r, hop_s, hop_r, far_s, far_r, halo_s, halo_r, extra_s, tile_s, tile_r, m_s, m_r,
):
    g = lax.axis_index("grp")
    p = lax.axis_index("pan")
    n = lax.axis_size("pan")
    core = lax.rem(g, 2)
    y_hi = g // 2
    z = lax.rem(p, 4)
    sib = g + 1 - 2 * core
    far = lax.rem(g + 2, 4)
    other_hi = 2 - 2 * y_hi
    wraps = jnp.logical_or(z == 0, z == 3)

    def across(pan):
        return pan + 4 - 8 * lax.rem(pan // 4, 2)

    before, after = lax.rem(p + n - 1, n), lax.rem(p + 1, n)
    inner = across(p)
    left, right = (g, before), (g, after)
    outer_to = (far, inner)
    inner_to = ((g, inner), (sib, inner))

    barrier = pltpu.get_barrier_semaphore()

    def greet(other):
        pl.semaphore_signal(barrier, inc=1, device_id=other, device_id_type=MESH)

    for other in ((sib, p), outer_to, *inner_to, left, right):
        greet(other)

    @pl.when(z == 0)
    def _():
        for who in (g, sib):
            greet((who, across(before)))

    @pl.when(z == 3)
    def _():
        for who in (g, sib):
            greet((who, across(after)))

    def one_hot(rows, cols, of_row, of_col):
        row = of_row(lax.broadcasted_iota(jnp.int32, (rows, cols), 0))
        return (row == of_col(lax.broadcasted_iota(jnp.int32, (rows, cols), 1))).astype(F32)

    eye = one_hot(CB, CB, lambda v: v, lambda v: v)
    lane = lax.broadcasted_iota(jnp.int32, (1, CB), 1)
    key_row = (dest_ref[...] * CB + lane).astype(F32)
    key_col = jnp.sum(eye * key_row, axis=1, keepdims=True)
    rank = jnp.sum((key_col < key_row).astype(F32), axis=0, keepdims=True)
    spread = one_hot(CB, T, lambda v: v, lambda v: v // ATOM)
    goal = jnp.sum(spread * jnp.sum(eye * rank, axis=1, keepdims=True), axis=0, keepdims=True)
    goal = goal * ATOM + (lax.broadcasted_iota(jnp.int32, (1, T), 1) % ATOM).astype(F32)

    def rows_for(group):
        want = (group * CHUNK + lax.broadcasted_iota(jnp.int32, (CHUNK, T), 0)).astype(F32)
        pick = (want == goal).astype(BF)
        return jnp.dot(pick, x_ref[...], preferred_element_type=F32).astype(BF)

    def rows_of(group, t=None):
        if t is None:
            return pl.ds(pl.multiple_of(group * CHUNK, CHUNK), CHUNK)
        return pl.ds(pl.multiple_of(group * CHUNK + CUTS[t], 16), CUTS[t + 1] - CUTS[t])

    sends = []

    def describe(src, dst, ss, rs, to):
        return pltpu.make_async_remote_copy(
            src_ref=src, dst_ref=dst, send_sem=ss, recv_sem=rs, device_id=to, device_id_type=MESH
        )

    def remote(*what):
        copy = describe(*what)
        copy.start()
        sends.append((None, lambda: copy))
        return copy

    def piece(t):
        return pl.ds(CUTS[t], CUTS[t + 1] - CUTS[t])

    def hop(d, t):
        return describe(for_far.at[d, piece(t)], transit.at[d, piece(t)], hop_s.at[d, t], hop_r.at[d, t], outer_to)

    for_far[0] = rows_for(other_hi)
    for_far[1] = rows_for(other_hi + 1)

    @pl.when(wraps)
    def _():
        pl.semaphore_wait(barrier, 8)

    @pl.when(jnp.logical_not(wraps))
    def _():
        pl.semaphore_wait(barrier, 6)

    def launch(t):
        for d in range(2):
            hop(d, t).start()
            sends.append((None, functools.partial(hop, d, t)))

    for t in range(PIECES):
        launch(t)
    mine[...] = jnp.zeros_like(mine)
    mine[:, : 3 * CB] = mask_ref[...].astype(F32)
    mask_in = (
        remote(mine, mask_l, m_s.at[0], m_r.at[0], right),
        remote(mine, mask_r, m_s.at[1], m_r.at[1], left),
    )
    for_sib[...] = rows_for(sib)
    from_sib = remote(for_sib, land.at[rows_of(g)], sib_s, sib_r, (sib, p))
    land[rows_of(g), :] = rows_for(g)

    right_cols, left_cols = pl.ds(T, 2 * T), pl.ds(0, 2 * T)
    slots = [rows_of(g), rows_of(sib)] + [rows_of(other_hi + c, t) for c in range(2) for t in range(PIECES)]

    def halo(side, slot):
        rows = slots[slot]
        if side == 0:
            return describe(land.at[rows, right_cols], a_hl.at[rows], halo_s.at[0, slot], halo_r.at[0, slot], right)
        return describe(land.at[rows, left_cols], a_hr.at[rows], halo_s.at[1, slot], halo_r.at[1, slot], left)

    def start_when(cond, copy):
        pl.when(cond)(copy.start)

    def onward(d, t):
        at = rows_of(far, t)
        return describe(transit.at[d, piece(t)], land.at[at], far_s.at[d, t], far_r.at[core, t], (y_hi * 2 + d, inner))

    def extra(side, d, t):
        at = rows_of(far, t)
        to = (y_hi * 2 + d, lax.rem(inner + (1 if side == 0 else n - 1), n))
        cols, dst = ((right_cols, a_hl), (left_cols, a_hr))[side]
        return describe(
            transit.at[d, piece(t), cols], dst.at[at], extra_s.at[side, d, t], halo_r.at[side, 2 + PIECES * core + t], to
        )

    def forward(d, t):
        hop(d, t).wait_recv()
        onward(d, t).start()
        start_when(z == 3, extra(0, d, t))
        start_when(z == 0, extra(1, d, t))

    def settle(c, t):
        slot = 2 + PIECES * c + t
        rows = slots[slot]
        describe(transit.at[0, piece(t)], land.at[rows], far_s.at[0, t], far_r.at[c, t], right).wait_recv()
        start_when(z != 3, halo(0, slot))
        start_when(z != 0, halo(1, slot))
        a_row[rows, :] = land[rows, :] * keep[rows, :]

    def expand(block, dst):
        rows = block.shape[0] * ATOM
        cols = block.shape[1] * ATOM
        up = one_hot(rows, CB, lambda v: v // ATOM, lambda v: v).astype(BF)
        over = one_hot(block.shape[1], cols, lambda v: v, lambda v: v // ATOM).astype(BF)
        tall = jnp.dot(up, block.astype(BF), preferred_element_type=F32)
        dst[...] = jnp.dot(tall.astype(BF), over, preferred_element_type=F32).astype(BF)

    def spread_near(slot):
        for side in range(2):
            halo(side, slot).start()

    spread_near(0)
    expand(mine[:, : 3 * CB], keep)
    from_sib.wait_recv()
    spread_near(1)
    mask_in[0].wait_recv()
    mask_in[1].wait_recv()
    expand(mask_l[:, CB : 3 * CB], keep_hl)
    expand(mask_r[:, : 2 * CB], keep_hr)
    for slot in range(2):
        a_row[slots[slot], :] = land[slots[slot], :] * keep[slots[slot], :]

    for t in range(PIECES):
        for k in range(2):
            forward(k, t)
            if t:
                settle(k, t - 1)
    for k in range(2):
        settle(k, PIECES - 1)

    for d in range(2):
        for t in range(PIECES):
            sends.append((None, functools.partial(onward, d, t)))
            sends.append((z == 3, functools.partial(extra, 0, d, t)))
            sends.append((z == 0, functools.partial(extra, 1, d, t)))
    for slot in [0, 1] + [2 + PIECES * c + t for t in range(PIECES) for c in range(2)]:
        for side, (dst, mask) in enumerate(((a_hl, keep_hl), (a_hr, keep_hr))):
            halo(side, slot).wait_recv()
            rows = slots[slot]
            dst[rows, :] = dst[rows, :] * mask[rows, :]
            away = None if slot < 2 else (z != 3, z != 0)[side]
            sends.append((away, functools.partial(halo, side, slot)))
    keep_um = keep_hl.at[:, pl.ds(T, T)]
    keep_lp = keep_hr.at[:, pl.ds(0, T)]

    def tile_of(ref, k):
        return ref.at[:, pl.ds(k * T, T)]

    def product(pairs, finish, after=None):
        for i in range(T // H):
            for j in range(T // H):
                acc = None
                for a, b in pairs:
                    part = jnp.dot(
                        a[i * H : (i + 1) * H, :], b[:, j * H : (j + 1) * H], preferred_element_type=F32
                    )
                    acc = part if acc is None else acc + part
                finish(i, j, acc)
            if after is not None:
                after(i)

    def to_factor(dst, mask, diagonal):
        def finish(i, j, acc):
            at = (slice(i * H, (i + 1) * H), slice(j * H, (j + 1) * H))
            value = acc * mask[at].astype(F32) * (-1.0 / (3.0 * T))
            if diagonal and i == j:
                same = lax.broadcasted_iota(jnp.int32, (H, H), 0) == lax.broadcasted_iota(jnp.int32, (H, H), 1)
                value = jnp.where(same, 3.0 + value, value)
            dst[at] = value.astype(BF)

        return finish

    def to_next(dst, mask, dtype):
        def finish(i, j, acc):
            at = (slice(i * H, (i + 1) * H), slice(j * H, (j + 1) * H))
            dst[at] = (0.5 * acc * mask[at].astype(F32)).astype(dtype)

        return finish

    k_l, k_d, k_u = (tile_of(keep, k) for k in range(3))

    def tiles(row, um_ref, lp_ref, dm_ref, dp_ref):
        return dict(l=tile_of(row, 0), d=tile_of(row, 1), u=tile_of(row, 2), um=um_ref, lp=lp_ref, dm=dm_ref, dp=dp_ref)

    a = tiles(a_row, tile_of(a_hl, 1), tile_of(a_hr, 0), tile_of(a_hl, 0), tile_of(a_hr, 1))
    b = tiles(b_row, tile_of(b_hl, 1), tile_of(b_hr, 0), tile_of(b_hl, 0), tile_of(b_hr, 1))
    f = tiles(f_row, f_um, f_lp, f_dm, f_dp)
    h = tiles(h_row, h_um, h_lp, h_dm, h_dp)

    def sender(k, src, from_left, from_right):
        def swap(side, i):
            half = pl.ds(i * H, H)
            dst, to = ((from_left, right), (from_right, left))[side]
            return describe(src.at[half], dst.at[half], tile_s.at[k, side, i], tile_r.at[k, side, i], to)

        def after(i):
            for side in range(2):
                swap(side, i).start()
                sends.append((None, functools.partial(swap, side, i)))

        def wait(side, i):
            swap(side, i).wait_recv()

        return after, wait

    def node(x, y):
        return [(x["d"], y["d"]), (x["u"], y["lp"]), (x["l"], y["um"])]

    def edge_um(x, y):
        return [(x["dm"], y["um"]), (x["um"], y["d"])]

    def edge_lp(x, y):
        return [(x["dp"], y["lp"]), (x["lp"], y["d"])]

    def edge_l(x, y):
        return [(x["d"], y["l"]), (x["l"], y["dm"])]

    def edge_u(x, y):
        return [(x["d"], y["u"]), (x["u"], y["dp"])]

    send_f, wait_f = sender(0, f["d"], f_dm, f_dp)
    send_b, wait_b = sender(1, b["d"], b["dm"], b["dp"])
    send_h, wait_h = sender(2, h["d"], h_dm, h_dp)

    product(node(a, a), to_factor(f["d"], k_d, True), send_f)
    product(edge_um(a, a), to_factor(f["um"], keep_um, False))
    product(edge_lp(a, a), to_factor(f["lp"], keep_lp, False))
    product(node(a, f), to_next(b["d"], k_d, BF), send_b)
    product(edge_l(a, a), to_factor(f["l"], k_l, False))
    product(edge_u(a, a), to_factor(f["u"], k_u, False))
    product(edge_um(a, f), to_next(b["um"], keep_um, BF))
    product(edge_lp(a, f), to_next(b["lp"], keep_lp, BF))

    wait_f(0, 0)
    wait_f(0, 1)
    product(edge_l(a, f), to_next(b["l"], k_l, BF))
    wait_f(1, 0)
    wait_f(1, 1)
    product(edge_u(a, f), to_next(b["u"], k_u, BF))

    product(node(b, b), to_factor(h["d"], k_d, True), send_h)
    wait_b(0, 0)
    wait_b(0, 1)
    product(edge_um(b, b), to_factor(h["um"], keep_um, False))
    product(edge_l(b, b), to_factor(h["l"], k_l, False))
    wait_b(1, 0)
    wait_b(1, 1)
    product(edge_lp(b, b), to_factor(h["lp"], keep_lp, False))
    product(edge_u(b, b), to_factor(h["u"], k_u, False))
    out_l, out_d, out_u = (tile_of(out_ref, k) for k in range(3))
    product(node(b, h), to_next(out_d, k_d, F32))

    def keep_sum(dst):
        def finish(i, j, acc):
            dst[i * H : (i + 1) * H, j * H : (j + 1) * H] = acc

        return finish

    def add_half(dst, x, y, q, mask):
        part = pl.ds(q * H, H)

        def finish(i, j, acc):
            at = (slice(i * H, (i + 1) * H), slice(j * H, (j + 1) * H))
            total = dst[at] + acc
            dst[at] = total if mask is None else 0.5 * total * mask[at].astype(F32)

        product([(x.at[:, part], y.at[part, :])], finish)

    product([(b["d"], h["l"])], keep_sum(out_l))
    product([(b["d"], h["u"])], keep_sum(out_u))
    for q in range(2):
        wait_h(0, q)
        add_half(out_l, b["l"], h_dm, q, k_l if q else None)
        wait_h(1, q)
        add_half(out_u, b["u"], h_dp, q, k_u if q else None)

    for cond, make in sends:
        if cond is None:
            make().wait_send()
        else:
            pl.when(cond)(make().wait_send)


def on_device(assembled, dest_group, block_mask):
    tile = pltpu.VMEM((T, T), BF)
    row = pltpu.VMEM((T, 3 * T), BF)
    pair = pltpu.VMEM((T, 2 * T), BF)
    dma = pltpu.SemaphoreType.DMA
    return pl.pallas_call(
        kernel,
        out_shape=jax.ShapeDtypeStruct((T, 3 * T), F32),
        in_specs=[
            pl.BlockSpec(memory_space=pltpu.VMEM),
            pl.BlockSpec(memory_space=pltpu.VMEM),
            pl.BlockSpec(memory_space=pltpu.VMEM),
        ],
        out_specs=pl.BlockSpec(memory_space=pltpu.VMEM),
        scratch_shapes=[
            pltpu.VMEM((2, CHUNK, 3 * T), BF), pltpu.VMEM((CHUNK, 3 * T), BF), pltpu.VMEM((2, CHUNK, 3 * T), BF), row,
            pltpu.VMEM((CB, 128), F32), pltpu.VMEM((CB, 128), F32), pltpu.VMEM((CB, 128), F32),
            row, pair, pair,
            row, pair, pair, row, tile, tile, tile, tile,
            row, pair, pair, row, tile, tile, tile, tile,
            dma, dma, dma((2, PIECES)), dma((2, PIECES)), dma((2, PIECES)), dma((2, PIECES)),
            dma((2, 2 + 2 * PIECES)), dma((2, 2 + 2 * PIECES)), dma((2, 2, PIECES)), dma((3, 2, 2)), dma((3, 2, 2)), dma((2,)), dma((2,)),
        ],
        compiler_params=pltpu.CompilerParams(
            collective_id=0, has_side_effects=True, vmem_limit_bytes=36 * 2**20
        ),
        cost_estimate=pl.CostEstimate(flops=40 * 2 * T**3, bytes_accessed=9 * T * T * 2, transcendentals=0),
        name="sign_steps",
    )(assembled, dest_group, block_mask)


def solution(mesh):
    spec = P(("grp", "pan"), None)
    return jax.shard_map(on_device, mesh=mesh, in_specs=(spec, spec, spec), out_specs=spec, check_vma=False)
```

time: 86.5 us -> 83.2 us (0.962)
  Pallas kernels: 82.4 us -> 78.6 us
    pallas_call x1, Pallas kernels: 82.4 us -> 78.6 us  [on_device(): pl.pallas_call(kernel, out_shape=jax.ShapeDtypeStruct((T, 3 * T), F32), i...]
    unnamed x1 -> x7, local copies, waits for them, and re-layouts: 3.76 us -> 4.42 us
where the time goes in v3:
time: 83.2 us; the launch traced here: 83 us
  Pallas kernels  78.6 us (94%)
  local copies, waits for them, and re-layouts  4.42 us (5%)
    pallas_call x1, Pallas kernels, on_device(): pl.pallas_call(kernel, out_shape=jax.ShapeDtypeStruct((T, 3 * T), F32), i...  78.6 us
    unnamed x7, local copies, waits for them, and re-layouts  4.42 us

profile of v3, /device:TPU:1, one launch (start us, length us, event | category | flops | bytes accessed | tf_op | source)
XLA Modules:
  0.0 83.0 jit_solution(6239001308167169588)
XLA Ops:
  0.0 0.0 copy-start
  0.0 1.4 %copy-done = bf16[512,1536]{1,0:T(8,128)(2,1)S(1)} copy-done((bf16[512,1536]{1,0:T(8,128)(2,1)S(1)}, bf16[512,1536]{1,0:T(8,128)(2,1)}, u32[]{:S(2)}) %copy-start) | copy-done | bytes 1572888
  1.4 0.0 copy-start.1
  1.4 0.7 copy-done.1
  2.1 0.0 copy-start.2
  2.1 0.7 copy-done.2
  2.8 78.6 %sign_steps.1 = f32[512,1536]{1,0:T(8,128)S(1)} custom-call(bf16[512,1536]{1,0:T(8,128)(2,1)S(1)} %copy-done, s32[1,8]{1,0:T(1,128)S(1)} %copy-done.2, s32[8,24]{1,0:T(8,128)S(1)} %copy-done.1), custom_call_target="tpu_custom_call" | custom-call | flops 10737418240 | bytes 4718592 | tf_op jit(solution)/shard_map/sign_steps/pallas_call | solution.py:364
  81.3 1.7 %copy.5 = f32[512,1536]{1,0:T(8,128)} copy(f32[512,1536]{1,0:T(8,128)S(1)} %sign_steps.1) | data formatting | bytes 6291456
Async XLA Ops:
  0.0 1.4 %copy-start = (bf16[512,1536]{1,0:T(8,128)(2,1)S(1)}, bf16[512,1536]{1,0:T(8,128)(2,1)}, u32[]{:S(2)}) copy-start(bf16[512,1536]{1,0:T(8,128)(2,1)} %x_ref.1) | copy-start | bytes 4718596
  1.4 0.7 copy-start.1
  2.1 0.7 copy-start.2

commit v4 on v3

--- a/solution.py
+++ b/solution.py
@@ -117,8 +117,10 @@
     def _():
         pl.semaphore_wait(barrier, 6)
 
+    turns = (core, 1 - core)
+
     def launch(t):
-        for d in range(2):
+        for d in turns:
             hop(d, t).start()
             sends.append((None, functools.partial(hop, d, t)))
 
@@ -137,8 +139,8 @@
     right_cols, left_cols = pl.ds(T, 2 * T), pl.ds(0, 2 * T)
     slots = [rows_of(g), rows_of(sib)] + [rows_of(other_hi + c, t) for c in range(2) for t in range(PIECES)]
 
-    def halo(side, slot):
-        rows = slots[slot]
+    def halo(side, slot, rows=None):
+        rows = slots[slot] if rows is None else rows
         if side == 0:
             return describe(land.at[rows, right_cols], a_hl.at[rows], halo_s.at[0, slot], halo_r.at[0, slot], right)
         return describe(land.at[rows, left_cols], a_hr.at[rows], halo_s.at[1, slot], halo_r.at[1, slot], left)
@@ -166,10 +168,10 @@
 
     def settle(c, t):
         slot = 2 + PIECES * c + t
-        rows = slots[slot]
+        rows = rows_of(other_hi + c, t)
         describe(transit.at[0, piece(t)], land.at[rows], far_s.at[0, t], far_r.at[c, t], right).wait_recv()
-        start_when(z != 3, halo(0, slot))
-        start_when(z != 0, halo(1, slot))
+        start_when(z != 3, halo(0, slot, rows))
+        start_when(z != 0, halo(1, slot, rows))
         a_row[rows, :] = land[rows, :] * keep[rows, :]
 
     def expand(block, dst):
@@ -197,11 +199,11 @@
 
     for t in range(PIECES):
         for k in range(2):
-            forward(k, t)
+            forward(turns[k], t)
             if t:
-                settle(k, t - 1)
+                settle(turns[k], t - 1)
     for k in range(2):
-        settle(k, PIECES - 1)
+        settle(turns[k], PIECES - 1)
 
     for d in range(2):
         for t in range(PIECES):
@@ -271,12 +273,16 @@
         def after(i):
             for side in range(2):
                 swap(side, i).start()
-                sends.append((None, functools.partial(swap, side, i)))
 
         def wait(side, i):
             swap(side, i).wait_recv()
 
-        return after, wait
+        def drain():
+            for i in range(T // H):
+                for side in range(2):
+                    swap(side, i).wait_send()
+
+        return after, wait, drain
 
     def node(x, y):
         return [(x["d"], y["d"]), (x["u"], y["lp"]), (x["l"], y["um"])]
@@ -293,18 +299,21 @@
     def edge_u(x, y):
         return [(x["d"], y["u"]), (x["u"], y["dp"])]
 
-    send_f, wait_f = sender(0, f["d"], f_dm, f_dp)
-    send_b, wait_b = sender(1, b["d"], b["dm"], b["dp"])
-    send_h, wait_h = sender(2, h["d"], h_dm, h_dp)
+    send_f, wait_f, drain_f = sender(0, f["d"], f_dm, f_dp)
+    send_b, wait_b, drain_b = sender(1, b["d"], b["dm"], b["dp"])
+    send_h, wait_h, drain_h = sender(2, h["d"], h_dm, h_dp)
 
     product(node(a, a), to_factor(f["d"], k_d, True), send_f)
     product(edge_um(a, a), to_factor(f["um"], keep_um, False))
     product(edge_lp(a, a), to_factor(f["lp"], keep_lp, False))
-    product(node(a, f), to_next(b["d"], k_d, BF), send_b)
+    product(node(a, f), to_next(b["d"], k_d, BF))
     product(edge_l(a, a), to_factor(f["l"], k_l, False))
     product(edge_u(a, a), to_factor(f["u"], k_u, False))
     product(edge_um(a, f), to_next(b["um"], keep_um, BF))
     product(edge_lp(a, f), to_next(b["lp"], keep_lp, BF))
+    drain_f()
+    send_b(0)
+    send_b(1)
 
     wait_f(0, 0)
     wait_f(0, 1)
@@ -349,6 +358,8 @@
         wait_h(1, q)
         add_half(out_u, b["u"], h_dp, q, k_u if q else None)
 
+    drain_b()
+    drain_h()
     for cond, make in sends:
         if cond is None:
             make().wait_send()

time: 83.2 us -> 82.7 us (level)
  no operation moved by 1% of the time
where the time goes in v4:
time: 82.7 us; the launch traced here: 82.3 us
  Pallas kernels  77.9 us (94%)
  local copies, waits for them, and re-layouts  4.42 us (5%)
    pallas_call x1, Pallas kernels, on_device(): pl.pallas_call(kernel, out_shape=jax.ShapeDtypeStruct((T, 3 * T), F32), i...  77.9 us
    unnamed x7, local copies, waits for them, and re-layouts  4.42 us

profile of v4, /device:TPU:1, one launch (start us, length us, event | category | flops | bytes accessed | tf_op | source)
XLA Modules:
  0.0 82.3 jit_solution(2853698884200188149)
XLA Ops:
  0.0 0.0 copy-start
  0.0 1.4 %copy-done = bf16[512,1536]{1,0:T(8,128)(2,1)S(1)} copy-done((bf16[512,1536]{1,0:T(8,128)(2,1)S(1)}, bf16[512,1536]{1,0:T(8,128)(2,1)}, u32[]{:S(2)}) %copy-start) | copy-done | bytes 1572888
  1.4 0.0 copy-start.1
  1.4 0.7 copy-done.1
  2.1 0.0 copy-start.2
  2.1 0.7 copy-done.2
  2.8 77.9 %sign_steps.1 = f32[512,1536]{1,0:T(8,128)S(1)} custom-call(bf16[512,1536]{1,0:T(8,128)(2,1)S(1)} %copy-done, s32[1,8]{1,0:T(1,128)S(1)} %copy-done.2, s32[8,24]{1,0:T(8,128)S(1)} %copy-done.1), custom_call_target="tpu_custom_call" | custom-call | flops 10737418240 | bytes 4718592 | tf_op jit(solution)/shard_map/sign_steps/pallas_call | solution.py:375
  80.6 1.7 %copy.5 = f32[512,1536]{1,0:T(8,128)} copy(f32[512,1536]{1,0:T(8,128)S(1)} %sign_steps.1) | data formatting | bytes 6291456
Async XLA Ops:
  0.0 1.4 %copy-start = (bf16[512,1536]{1,0:T(8,128)(2,1)S(1)}, bf16[512,1536]{1,0:T(8,128)(2,1)}, u32[]{:S(2)}) copy-start(bf16[512,1536]{1,0:T(8,128)(2,1)} %x_ref.1) | copy-start | bytes 4718596
  1.4 0.7 copy-start.1
  2.1 0.7 copy-start.2

commit v5 on v4

--- a/solution.py
+++ b/solution.py
@@ -322,7 +322,10 @@
     wait_f(1, 1)
     product(edge_u(a, f), to_next(b["u"], k_u, BF))
 
-    product(node(b, b), to_factor(h["d"], k_d, True), send_h)
+    product(node(b, b), to_factor(h["d"], k_d, True))
+    drain_b()
+    send_h(0)
+    send_h(1)
     wait_b(0, 0)
     wait_b(0, 1)
     product(edge_um(b, b), to_factor(h["um"], keep_um, False))
@@ -358,7 +361,6 @@
         wait_h(1, q)
         add_half(out_u, b["u"], h_dp, q, k_u if q else None)
 
-    drain_b()
     drain_h()
     for cond, make in sends:
         if cond is None:

time: 82.7 us -> 82.7 us (level)
  no operation moved by 1% of the time
where the time goes in v5:
time: 82.7 us; the launch traced here: 81.7 us
  Pallas kernels  77.3 us (93%)
  local copies, waits for them, and re-layouts  4.42 us (5%)
    pallas_call x1, Pallas kernels, on_device(): pl.pallas_call(kernel, out_shape=jax.ShapeDtypeStruct((T, 3 * T), F32), i...  77.3 us
    unnamed x7, local copies, waits for them, and re-layouts  4.42 us

profile of v5, /device:TPU:1, one launch (start us, length us, event | category | flops | bytes accessed | tf_op | source)
XLA Modules:
  0.0 81.7 jit_solution(8715744201903704232)
XLA Ops:
  0.0 0.0 copy-start
  0.0 1.4 %copy-done = bf16[512,1536]{1,0:T(8,128)(2,1)S(1)} copy-done((bf16[512,1536]{1,0:T(8,128)(2,1)S(1)}, bf16[512,1536]{1,0:T(8,128)(2,1)}, u32[]{:S(2)}) %copy-start) | copy-done | bytes 1572888
  1.4 0.0 copy-start.1
  1.4 0.7 copy-done.1
  2.1 0.0 copy-start.2
  2.1 0.7 copy-done.2
  2.8 77.3 %sign_steps.1 = f32[512,1536]{1,0:T(8,128)S(1)} custom-call(bf16[512,1536]{1,0:T(8,128)(2,1)S(1)} %copy-done, s32[1,8]{1,0:T(1,128)S(1)} %copy-done.2, s32[8,24]{1,0:T(8,128)S(1)} %copy-done.1), custom_call_target="tpu_custom_call" | custom-call | flops 10737418240 | bytes 4718592 | tf_op jit(solution)/shard_map/sign_steps/pallas_call | solution.py:377
  80.1 1.7 %copy.5 = f32[512,1536]{1,0:T(8,128)} copy(f32[512,1536]{1,0:T(8,128)S(1)} %sign_steps.1) | data formatting | bytes 6291456
Async XLA Ops:
  0.0 1.4 %copy-start = (bf16[512,1536]{1,0:T(8,128)(2,1)S(1)}, bf16[512,1536]{1,0:T(8,128)(2,1)}, u32[]{:S(2)}) copy-start(bf16[512,1536]{1,0:T(8,128)(2,1)} %x_ref.1) | copy-start | bytes 4718596
  1.4 0.7 copy-start.1
  2.1 0.7 copy-start.2
